TPU v7x, 256 devices: a whole 4x4x8 slice. The times are simulated.
256 devices in a mesh: variant: 8 (over x, core), mesh: 32 (over z, y).
Axes of the slice: x: 4, y: 4, z: 8, core: 2. Of those that a mesh axis runs over, the one named last changes fastest.
Arguments:
- snapshots: float32 [8, 64, 524288], P('variant', None, 'mesh'), may hold values from -12 to 12, as said below
- ref_index: int32 [1], replicated, may hold values from 0 to 7
- weight_codes: int32 [8], replicated, may hold values from 1 to 16
Outputs:
- new_basis: float32 [64, 524288], P(None, 'mesh')
Inputs may be any that keep to these rules, and one draw needn't show every extreme that they name: `snapshots`: each variant's snapshot matrix has full rank 64, and the principal angles between any two variants' spans have tangents below 0.8.
All inputs are finite; a program needn't handle non-finite values.
Results may differ from a plain program's by a relative error of at most 0.0001.
Values sent between devices are 32-bit elements; how exact they have to be, the bound alone decides.
A program may use at most 64 MiB of HBM per device.

v0:
```python
import math
import jax
import jax.numpy as jnp
from jax import lax
from jax.sharding import Mesh
from jax.sharding import PartitionSpec as P

VARIANT = ("variant_0", "variant_1")
highest = lax.Precision.HIGHEST
atan_coeffs = [(-1.0) ** k / (2 * k + 1) for k in range(24)]
cos_coeffs = [(-1.0) ** k / math.factorial(2 * k) for k in range(24)]
sin_coeffs = [(-1.0) ** k / math.factorial(2 * k + 1) for k in range(24)]


def from_everyone(x, axis):
    count = lax.axis_size(axis)
    return lax.all_to_all(jnp.broadcast_to(x[None], (count, *x.shape)), axis, 0, 0, tiled=True)


def of_everyone(x, axis):
    everything = from_everyone(x, axis)
    return jnp.sum(everything, axis=0)


def spread(x, axes, root):
    x = jnp.where(lax.axis_index(axes) == root, x, jnp.zeros_like(x))
    for axis in axes:
        x = lax.psum(x, axis)
    return x


def product(left, right):
    return jnp.dot(left, right, precision=highest, preferred_element_type=jnp.float32)


def series(matrix, coeffs):
    eye = jnp.eye(matrix.shape[0], dtype=jnp.float32)
    total = coeffs[-1] * eye
    for coeff in reversed(coeffs[:-1]):
        total = coeff * eye + product(matrix, total)
    return total


def inverse(matrix):
    factor = jnp.linalg.cholesky(product(matrix.T, matrix))
    return jax.scipy.linalg.cho_solve((factor, True), matrix.T)


def on_device(snapshots, ref_index, weight_codes):
    own_snap = snapshots[0]
    root = ref_index[0]
    codes = weight_codes.astype(jnp.float32)
    weight = codes[lax.axis_index(VARIANT)] / jnp.sum(codes)
    eye = jnp.eye(own_snap.shape[0], dtype=jnp.float32)
    scale = jnp.float32(math.sqrt(own_snap.shape[1] * lax.axis_size("mesh")))
    gram_own = of_everyone(product(own_snap, own_snap.T), "mesh")
    lower_own = jnp.linalg.cholesky(gram_own)
    base_own = jax.scipy.linalg.solve_triangular(lower_own, own_snap, lower=True)
    base_ref = spread(base_own, VARIANT, root)
    correlation = of_everyone(product(base_ref, base_own.T), "mesh")
    minv = inverse(correlation)
    tangent = product(minv.T, base_own) - base_ref
    tangent_gram = product(minv.T, minv) - eye
    term = weight * product(series(tangent_gram, atan_coeffs), tangent)
    blended = lax.psum(term, VARIANT)
    energy = of_everyone(product(blended, blended.T), "mesh")
    mixed = product(series(energy, cos_coeffs), base_ref) + product(
        series(energy, sin_coeffs), blended
    )
    return mixed * scale


def solution(mesh):
    finer = Mesh(mesh.devices.reshape(4, 2, mesh.shape["mesh"]), ("variant_0", "variant_1", "mesh"))
    placed = (P(VARIANT, None, "mesh"), P(), P())
    return jax.shard_map(
        on_device, mesh=finer, in_specs=placed, out_specs=P(None, "mesh"), check_vma=False
    )
```

profile of v0, /device:TPU:7, one launch (start us, length us, event | category | flops | bytes accessed | tf_op | source)
XLA Modules:
  0.0 408.7 jit_solution(8007824990110213597)
XLA Ops:
  6.5 6.9 %fusion.3 = f32[64,64]{1,0:T(8,128)S(1)} fusion(f32[1,64,16384]{2,1,0:T(8,128)} %param.4), kind=kOutput, calls=%fused_computation.6 | convolution fusion | flops 805306368 | bytes 4210688 | tf_op jit(solution)/shard_map/dot_general | solution.py:33
  13.6 1.4 reshape.19
  15.0 11.2 %all-to-all-start = ((f32[32,1,4096]{2,1,0:T(1,128)}), f32[32,1,4096]{2,1,0:T(1,128)S(1)}, u32[]{:S(2)}, u32[]{:S(2)}) async-start(f32[32,1,4096]{2,1,0:T(1,128)} %reshape.19), calls=%async_computation | async-start | bytes 1048576 | tf_op jit(solution)/shard_map/all_to_all | solution.py:17
  27.3 15.3 %all-to-all-done = f32[32,1,4096]{2,1,0:T(1,128)S(1)} async-done(((f32[32,1,4096]{2,1,0:T(1,128)}), f32[32,1,4096]{2,1,0:T(1,128)S(1)}, u32[]{:S(2)}, u32[]{:S(2)}) %all-to-all-start) | async-done | bytes 524320 | tf_op jit(solution)/shard_map/all_to_all | solution.py:17
  43.1 1.9 reduce.4
  45.5 5.8 %cholesky.44 = f32[64,64]{1,0:T(8,128)S(1)} custom-call(f32[64,64]{1,0:T(8,128)S(1)} %fusion.15), custom_call_target="Cholesky" | custom-call | tf_op jit(solution)/shard_map/jit(cholesky)/cholesky | solution.py:57
  51.4 0.6 compare_reduce_fusion.1
  52.1 0.7 fusion.7
  52.7 4.9 %custom-call.13 = f32[1,64,64]{1,2,0:T(8,128)S(1)} custom-call(f32[1,64,64]{2,1,0:T(8,128)S(1)} %fusion.7), custom_call_target="InvertDiagBlocksLowerTriangular" | custom-call | tf_op jit(solution)/shard_map/jit(_solve_triangular)/triangular_solve | solution.py:58
  57.6 9.3 %broadcast_select_fusion = (f32[64,16384]{1,0:T(8,128)}, f32[64,16384]{1,0:T(8,128)}) fusion(pred[]{:T(512)S(6)} %eq.142, f32[1,64,16384]{2,1,0:T(8,128)} %param.4, f32[1,64,64]{1,2,0:T(8,128)S(1)} %custom-call.13), kind=kOutput, calls=%fused_computation.8 | convolution fusion | flops 806354944 | bytes 12599297 | tf_op jit(solution)/shard_map/jit(_solve_triangular)/triangular_solve | solution.py:58
  67.0 94.0 %all-reduce.4.cloned.1.call-done = f32[64,16384]{1,0:T(8,128)} async-done(((f32[64,16384]{1,0:T(8,128)}), f32[64,16384]{1,0:T(8,128)}) %all-reduce.4.cloned.1.call-update) | async-done | bytes 4194320 | tf_op jit(solution)/shard_map/psum | solution.py:28
  161.0 44.4 %all-reduce.6.cloned.1.call-done = f32[64,16384]{1,0:T(8,128)} async-done(((f32[64,16384]{1,0:T(8,128)}), f32[64,16384]{1,0:T(8,128)}) %all-reduce.6.cloned.1.call-update) | async-done | bytes 4194320 | tf_op jit(solution)/shard_map/psum | solution.py:28
  205.4 6.9 %fusion.35 = f32[64,64]{1,0:T(8,128)S(1)} fusion(f32[64,16384]{1,0:T(8,128)} %all-reduce.6.cloned.1.call-done, f32[64,16384]{1,0:T(8,128)} %get-tuple-element.7), kind=kOutput, calls=%fused_computation.114 | convolution fusion | flops 805306368 | bytes 8404992 | tf_op jit(solution)/shard_map/dot_general | solution.py:33
  212.5 1.4 reshape.21
  213.9 9.6 %all-to-all-start.1 = ((f32[32,1,4096]{2,1,0:T(1,128)}), f32[32,1,4096]{2,1,0:T(1,128)S(1)}, u32[]{:S(2)}, u32[]{:S(2)}) async-start(f32[32,1,4096]{2,1,0:T(1,128)} %reshape.21), calls=%async_computation.1 | async-start | bytes 1048576 | tf_op jit(solution)/shard_map/all_to_all | solution.py:17
  223.6 0.6 dynamic_slice.3
  224.1 0.6 convert_reduce_fusion
  226.0 14.2 %all-to-all-done.1 = f32[32,1,4096]{2,1,0:T(1,128)S(1)} async-done(((f32[32,1,4096]{2,1,0:T(1,128)}), f32[32,1,4096]{2,1,0:T(1,128)S(1)}, u32[]{:S(2)}, u32[]{:S(2)}) %all-to-all-start.1) | async-done | bytes 524320 | tf_op jit(solution)/shard_map/all_to_all | solution.py:17
  240.2 1.9 reduce.5
  242.9 5.8 %cholesky.55 = f32[64,64]{1,0:T(8,128)S(1)} custom-call(f32[64,64]{1,0:T(8,128)S(1)} %fusion.13), custom_call_target="Cholesky" | custom-call | tf_op jit(solution)/shard_map/jit(cholesky)/cholesky | solution.py:45
  248.8 0.6 compare_reduce_fusion
  249.4 0.7 fusion.8
  250.1 4.9 %custom-call.14 = f32[1,64,64]{1,2,0:T(8,128)S(1)} custom-call(f32[1,64,64]{2,1,0:T(8,128)S(1)} %fusion.8), custom_call_target="InvertDiagBlocksLowerTriangular" | custom-call | tf_op jit(solution)/shard_map/jit(_cho_solve)/triangular_solve | solution.py:46
  259.5 7.2 %convolution_subtract_fusion = f32[64,16384]{1,0:T(8,128)S(1)} fusion(f32[64,16384]{1,0:T(8,128)} %all-reduce.6.cloned.1.call-done, f32[64,64]{1,0:T(8,128)S(1)} %fusion.9, f32[64,16384]{1,0:T(8,128)} %get-tuple-element.7), kind=kOutput, calls=%fused_computation.3 | convolution fusion | flops 806354944 | bytes 12599296 | tf_op jit(solution)/shard_map/dot_general | solution.py:33
  266.7 5.4 %convolution_multiply_fusion = f32[64,16384]{1,0:T(8,128)} fusion(f32[64,64]{1,0:T(8,128)S(1)} %convolution_add_fusion.40, f32[64,16384]{1,0:T(8,128)S(1)} %convolution_subtract_fusion, f32[]{:T(128)S(6)} %div.9), kind=kOutput, calls=%fused_computation.2 | convolution fusion | flops 806354944 | bytes 8404996 | tf_op jit(solution)/shard_map/dot_general | solution.py:33
  272.1 74.9 %all-reduce.8.cloned.1.call-done = f32[64,16384]{1,0:T(8,128)} async-done(((f32[64,16384]{1,0:T(8,128)}), f32[64,16384]{1,0:T(8,128)}) %all-reduce.8.cloned.1.call-update) | async-done | bytes 4194320 | tf_op jit(solution)/shard_map/psum | solution.py:65
  347.0 6.9 %fusion.37 = f32[64,64]{1,0:T(8,128)S(1)} fusion(f32[64,16384]{1,0:T(8,128)} %all-reduce.8.cloned.1.call-done), kind=kOutput, calls=%fused_computation.116 | convolution fusion | flops 805306368 | bytes 4210688 | tf_op jit(solution)/shard_map/dot_general | solution.py:33
  354.0 0.7 reshape.23
  354.7 26.7 %all_to_all.15 = f32[32,1,4096]{2,1,0:T(1,128)S(1)} all-to-all(f32[32,1,4096]{2,1,0:T(1,128)S(1)} %reshape.23), channel_id=1, replica_groups=mesh['variant_0'=4,'variant_1'=2,'mesh'=32] {'mesh'}, dimensions={0} | all-to-all | bytes 1048576 | tf_op jit(solution)/shard_map/all_to_all | solution.py:17
  381.4 1.9 reduce.6
  390.9 5.6 %fusion.40 = f32[64,16384]{1,0:T(8,128)S(1)} fusion(f32[64,64]{1,0:T(8,128)S(1)} %convolution_add_fusion.20, f32[64,16384]{1,0:T(8,128)} %all-reduce.6.cloned.1.call-done), kind=kOutput, calls=%fused_computation.119 | convolution fusion | flops 805306368 | bytes 8404992 | tf_op jit(solution)/shard_map/dot_general | solution.py:33
  396.5 5.4 %fusion = f32[64,16384]{1,0:T(8,128)} fusion(f32[64,16384]{1,0:T(8,128)S(1)} %fusion.40, f32[64,64]{1,0:T(8,128)S(1)} %convolution_add_fusion.1, f32[64,16384]{1,0:T(8,128)S(1)} %copy-done), kind=kOutput, calls=%fused_computation.1 | convolution fusion | flops 807403520 | bytes 12599296 | tf_op jit(solution)/shard_map/dot_general | solution.py:33
  (96 shorter events, 14.5 us)
Async XLA Ops:
  15.0 27.5 %all-to-all-start = ((f32[32,1,4096]{2,1,0:T(1,128)}), f32[32,1,4096]{2,1,0:T(1,128)S(1)}, u32[]{:S(2)}, u32[]{:S(2)}) async-start(f32[32,1,4096]{2,1,0:T(1,128)} %reshape.19), calls=%async_computation | async-start | bytes 1048576 | tf_op jit(solution)/shard_map/all_to_all | solution.py:17
  26.3 134.7 %all-reduce.4.cloned.1.call-start = ((), (), s32[]{:S(2)}) async-start(), calls=%async_computation.3 | async-start | bytes 8388608 | tf_op jit(solution)/shard_map/psum | solution.py:28
  66.9 138.5 %all-reduce.6.cloned.1.call-start = ((), (), s32[]{:S(2)}) async-start(), calls=%async_computation.4 | async-start | bytes 8388608 | tf_op jit(solution)/shard_map/psum | solution.py:28
  205.4 18.2 %copy-start.1 = (s32[8]{0:T(128)S(1)}, s32[8]{0:T(128)}, u32[]{:S(2)}) copy-start(s32[8]{0:T(128)} %param.6) | copy-start | bytes 100
  213.9 26.2 %all-to-all-start.1 = ((f32[32,1,4096]{2,1,0:T(1,128)}), f32[32,1,4096]{2,1,0:T(1,128)S(1)}, u32[]{:S(2)}, u32[]{:S(2)}) async-start(f32[32,1,4096]{2,1,0:T(1,128)} %reshape.21), calls=%async_computation.1 | async-start | bytes 1048576 | tf_op jit(solution)/shard_map/all_to_all | solution.py:17
  223.5 123.5 %all-reduce.8.cloned.1.call-start = ((), (), s32[]{:S(2)}) async-start(), calls=%async_computation.5 | async-start | bytes 8388608 | tf_op jit(solution)/shard_map/psum | solution.py:65
  390.9 5.6 %copy-start = (f32[64,16384]{1,0:T(8,128)S(1)}, f32[64,16384]{1,0:T(8,128)}, u32[]{:S(2)}) copy-start(f32[64,16384]{1,0:T(8,128)} %all-reduce.8.cloned.1.call-done) | copy-start | bytes 12582916
Sparse Core Ops, SparseCore 0:
  67.1 93.8 all-reduce.3
  163.9 41.4 all-reduce.5
  272.2 74.6 all-reduce.7
where the time goes:
time: 413 us; the launch traced here: 409 us
  waiting for transfers between devices  243 us (59%)
  matrix products  65.1 us (16%)
  other arithmetic  30.6 us (7%)
  blocking collectives  26.7 us (6%)
  starting transfers between devices  21.2 us (5%)
  between operations  16 us (4%)
  local copies, waits for them, and re-layouts  6.37 us (2%)
    psum x2, waiting for transfers between devices, spread(): x = lax.psum(x, axis)  138 us
    psum x1, waiting for transfers between devices, on_device(): blended = lax.psum(term, VARIANT)  74.9 us
    dot_general x74, matrix products, product(): jnp.dot(left, right, precision=highest, preferred_element_type=jnp.float32)  55.4 us
    all_to_all x2, waiting for transfers between devices, from_everyone(): lax.all_to_all(jnp.broadcast_to(x[None], (count, *x.shape)), axis, 0, 0,...  29.4 us
    all_to_all x1, blocking collectives, from_everyone(): lax.all_to_all(jnp.broadcast_to(x[None], (count, *x.shape)), axis, 0, 0,...  26.7 us
    all_to_all x2, starting transfers between devices, from_everyone(): lax.all_to_all(jnp.broadcast_to(x[None], (count, *x.shape)), axis, 0, 0,...  20.8 us
    another operation x1, matrix products, on_device(): jax.scipy.linalg.solve_triangular(lower_own, own_snap, lower=True)  9.3 us
  transfers between devices with their start and end apart: 5, of which 5 were waited for; matrix products, arithmetic and copies ran while one was open for 0% of the time, Pallas kernels for 0%

commit v1 on v0

--- a/solution.py
+++ b/solution.py
@@ -25,7 +25,7 @@
 def spread(x, axes, root):
     x = jnp.where(lax.axis_index(axes) == root, x, jnp.zeros_like(x))
     for axis in axes:
-        x = lax.psum(x, axis)
+        x = jnp.sum(lax.all_gather(x, axis), axis=0)
     return x
 
 

time: 413 us -> 472 us (1.14)
  waiting for transfers between devices: 243 us -> 285 us
  other arithmetic: 30.6 us -> 46.5 us
    all_gather x0 -> x2, waiting for transfers between devices: none -> 181 us  [spread(): x = jnp.sum(lax.all_gather(x, axis), axis=0)]
    psum x2 -> x0, waiting for transfers between devices: 138 us -> none  [spread(): x = lax.psum(x, axis)]
    reduce_sum x0 -> x2, other arithmetic: none -> 15.8 us  [spread(): x = jnp.sum(lax.all_gather(x, axis), axis=0)]
where the time goes in v1:
time: 472 us; the launch traced here: 468 us
  waiting for transfers between devices  285 us (60%)
  matrix products  65.2 us (14%)
  other arithmetic  46.5 us (10%)
  blocking collectives  26.7 us (6%)
  starting transfers between devices  21.9 us (5%)
  between operations  16.1 us (3%)
  local copies, waits for them, and re-layouts  6.48 us (1%)
    all_gather x2, waiting for transfers between devices, spread(): x = jnp.sum(lax.all_gather(x, axis), axis=0)  181 us
    psum x1, waiting for transfers between devices, on_device(): blended = lax.psum(term, VARIANT)  74.8 us
    dot_general x74, matrix products, product(): jnp.dot(left, right, precision=highest, preferred_element_type=jnp.float32)  55.4 us
    all_to_all x2, waiting for transfers between devices, from_everyone(): lax.all_to_all(jnp.broadcast_to(x[None], (count, *x.shape)), axis, 0, 0,...  29.1 us
    all_to_all x1, blocking collectives, from_everyone(): lax.all_to_all(jnp.broadcast_to(x[None], (count, *x.shape)), axis, 0, 0,...  26.7 us
    all_to_all x2, starting transfers between devices, from_everyone(): lax.all_to_all(jnp.broadcast_to(x[None], (count, *x.shape)), axis, 0, 0,...  20.8 us
    reduce_sum x2, other arithmetic, spread(): x = jnp.sum(lax.all_gather(x, axis), axis=0)  15.8 us
  transfers between devices with their start and end apart: 5, of which 5 were waited for; matrix products, arithmetic and copies ran while one was open for 0% of the time, Pallas kernels for 0%

profile of v1, /device:TPU:7, one launch (start us, length us, event | category | flops | bytes accessed | tf_op | source)
XLA Modules:
  0.0 467.7 jit_solution(15681664673907301742)
XLA Ops:
  6.5 6.9 %fusion.3 = f32[64,64]{1,0:T(8,128)S(1)} fusion(f32[1,64,16384]{2,1,0:T(8,128)} %param.4), kind=kOutput, calls=%fused_computation.6 | convolution fusion | flops 805306368 | bytes 4210688 | tf_op jit(solution)/shard_map/dot_general | solution.py:33
  13.6 1.4 reshape.21
  15.0 11.2 %all-to-all-start = ((f32[32,1,4096]{2,1,0:T(1,128)}), f32[32,1,4096]{2,1,0:T(1,128)S(1)}, u32[]{:S(2)}, u32[]{:S(2)}) async-start(f32[32,1,4096]{2,1,0:T(1,128)} %reshape.21), calls=%async_computation | async-start | bytes 1048576 | tf_op jit(solution)/shard_map/all_to_all | solution.py:17
  27.3 15.3 %all-to-all-done = f32[32,1,4096]{2,1,0:T(1,128)S(1)} async-done(((f32[32,1,4096]{2,1,0:T(1,128)}), f32[32,1,4096]{2,1,0:T(1,128)S(1)}, u32[]{:S(2)}, u32[]{:S(2)}) %all-to-all-start) | async-done | bytes 524320 | tf_op jit(solution)/shard_map/all_to_all | solution.py:17
  43.1 1.9 reduce.4
  45.6 5.8 %cholesky.44 = f32[64,64]{1,0:T(8,128)S(1)} custom-call(f32[64,64]{1,0:T(8,128)S(1)} %fusion.15), custom_call_target="Cholesky" | custom-call | tf_op jit(solution)/shard_map/jit(cholesky)/cholesky | solution.py:57
  52.1 0.7 fusion.7
  52.7 4.9 %custom-call.13 = f32[1,64,64]{1,2,0:T(8,128)S(1)} custom-call(f32[1,64,64]{2,1,0:T(8,128)S(1)} %fusion.7), custom_call_target="InvertDiagBlocksLowerTriangular" | custom-call | tf_op jit(solution)/shard_map/jit(_solve_triangular)/triangular_solve | solution.py:58
  57.6 9.3 %broadcast_select_fusion = (f32[64,16384]{1,0:T(8,128)}, f32[64,16384]{1,0:T(8,128)}) fusion(pred[]{:T(512)S(6)} %eq.142, f32[1,64,16384]{2,1,0:T(8,128)} %param.4, f32[1,64,64]{1,2,0:T(8,128)S(1)} %custom-call.13), kind=kOutput, calls=%fused_computation.8 | convolution fusion | flops 806354944 | bytes 12599297 | tf_op jit(solution)/shard_map/jit(_solve_triangular)/triangular_solve | solution.py:58
  67.5 152.3 %all-gather.5.cloned.1.call-done = f32[256,16384]{1,0:T(8,128)} async-done(((f32[64,16384]{1,0:T(8,128)}), f32[256,16384]{1,0:T(8,128)}) %all-gather.5.cloned.1.call-update) | async-done | bytes 16777232 | tf_op jit(solution)/shard_map/all_gather | solution.py:28
  219.8 9.3 %reduce_sum.56 = f32[64,16384]{1,0:T(8,128)} reduce(f32[4,64,16384]{2,1,0:T(8,128)} %bitcast.178, f32[]{:T(128)} %constant.189.clone.1), dimensions={0}, to_apply=%region_4.6 | reduce | flops 3145728 | bytes 20971524 | tf_op jit(solution)/shard_map/reduce_sum | solution.py:28
  229.2 28.5 %all-gather.7.cloned.1.call-done = f32[128,16384]{1,0:T(8,128)} async-done(((f32[64,16384]{1,0:T(8,128)}), f32[128,16384]{1,0:T(8,128)}) %all-gather.7.cloned.1.call-update) | async-done | bytes 8388624 | tf_op jit(solution)/shard_map/all_gather | solution.py:28
  257.7 6.5 %reduce_sum.57 = f32[64,16384]{1,0:T(8,128)} reduce(f32[2,64,16384]{2,1,0:T(8,128)} %bitcast.179, f32[]{:T(128)} %constant.189.clone.1), dimensions={0}, to_apply=%region_5.7 | reduce | flops 1048576 | bytes 12582916 | tf_op jit(solution)/shard_map/reduce_sum | solution.py:28
  264.2 6.9 %fusion.35 = f32[64,64]{1,0:T(8,128)S(1)} fusion(f32[64,16384]{1,0:T(8,128)} %reduce_sum.57, f32[64,16384]{1,0:T(8,128)} %get-tuple-element.7), kind=kOutput, calls=%fused_computation.114 | convolution fusion | flops 805306368 | bytes 8404992 | tf_op jit(solution)/shard_map/dot_general | solution.py:33
  271.3 1.4 reshape.23
  272.7 9.6 %all-to-all-start.1 = ((f32[32,1,4096]{2,1,0:T(1,128)}), f32[32,1,4096]{2,1,0:T(1,128)S(1)}, u32[]{:S(2)}, u32[]{:S(2)}) async-start(f32[32,1,4096]{2,1,0:T(1,128)} %reshape.23), calls=%async_computation.1 | async-start | bytes 1048576 | tf_op jit(solution)/shard_map/all_to_all | solution.py:17
  282.5 0.7 dynamic_slice.3
  285.1 13.9 %all-to-all-done.1 = f32[32,1,4096]{2,1,0:T(1,128)S(1)} async-done(((f32[32,1,4096]{2,1,0:T(1,128)}), f32[32,1,4096]{2,1,0:T(1,128)S(1)}, u32[]{:S(2)}, u32[]{:S(2)}) %all-to-all-start.1) | async-done | bytes 524320 | tf_op jit(solution)/shard_map/all_to_all | solution.py:17
  299.0 1.9 reduce.5
  301.7 5.8 %cholesky.55 = f32[64,64]{1,0:T(8,128)S(1)} custom-call(f32[64,64]{1,0:T(8,128)S(1)} %fusion.13), custom_call_target="Cholesky" | custom-call | tf_op jit(solution)/shard_map/jit(cholesky)/cholesky | solution.py:45
  307.6 0.7 compare_reduce_fusion
  308.3 0.7 fusion.8
  309.0 4.9 %custom-call.14 = f32[1,64,64]{1,2,0:T(8,128)S(1)} custom-call(f32[1,64,64]{2,1,0:T(8,128)S(1)} %fusion.8), custom_call_target="InvertDiagBlocksLowerTriangular" | custom-call | tf_op jit(solution)/shard_map/jit(_cho_solve)/triangular_solve | solution.py:46
  314.3 7.2 %convolution_subtract_fusion = f32[64,16384]{1,0:T(8,128)S(1)} fusion(f32[64,16384]{1,0:T(8,128)} %reduce_sum.57, f32[64,64]{1,0:T(8,128)S(1)} %fusion.9, f32[64,16384]{1,0:T(8,128)} %get-tuple-element.7), kind=kOutput, calls=%fused_computation.3 | convolution fusion | flops 806354944 | bytes 12599296 | tf_op jit(solution)/shard_map/dot_general | solution.py:33
  325.7 5.4 %convolution_multiply_fusion = f32[64,16384]{1,0:T(8,128)} fusion(f32[64,64]{1,0:T(8,128)S(1)} %convolution_add_fusion.40, f32[64,16384]{1,0:T(8,128)S(1)} %convolution_subtract_fusion, f32[]{:T(128)S(6)} %div.9), kind=kOutput, calls=%fused_computation.2 | convolution fusion | flops 806354944 | bytes 8404996 | tf_op jit(solution)/shard_map/dot_general | solution.py:33
  331.1 74.8 %all-reduce.2.cloned.1.call-done = f32[64,16384]{1,0:T(8,128)} async-done(((f32[64,16384]{1,0:T(8,128)}), f32[64,16384]{1,0:T(8,128)}) %all-reduce.2.cloned.1.call-update) | async-done | bytes 4194320 | tf_op jit(solution)/shard_map/psum | solution.py:65
  406.0 6.9 %fusion.37 = f32[64,64]{1,0:T(8,128)S(1)} fusion(f32[64,16384]{1,0:T(8,128)} %all-reduce.2.cloned.1.call-done), kind=kOutput, calls=%fused_computation.116 | convolution fusion | flops 805306368 | bytes 4210688 | tf_op jit(solution)/shard_map/dot_general | solution.py:33
  413.0 0.7 reshape.25
  413.7 26.7 %all_to_all.15 = f32[32,1,4096]{2,1,0:T(1,128)S(1)} all-to-all(f32[32,1,4096]{2,1,0:T(1,128)S(1)} %reshape.25), channel_id=1, replica_groups=mesh['variant_0'=4,'variant_1'=2,'mesh'=32] {'mesh'}, dimensions={0} | all-to-all | bytes 1048576 | tf_op jit(solution)/shard_map/all_to_all | solution.py:17
  440.4 1.9 reduce.6
  446.9 5.6 %fusion.40 = f32[64,16384]{1,0:T(8,128)S(1)} fusion(f32[64,64]{1,0:T(8,128)S(1)} %convolution_add_fusion.20, f32[64,16384]{1,0:T(8,128)} %reduce_sum.57), kind=kOutput, calls=%fused_computation.119 | convolution fusion | flops 805306368 | bytes 8404992 | tf_op jit(solution)/shard_map/dot_general | solution.py:33
  455.5 5.4 %fusion = f32[64,16384]{1,0:T(8,128)} fusion(f32[64,16384]{1,0:T(8,128)S(1)} %fusion.40, f32[64,64]{1,0:T(8,128)S(1)} %convolution_add_fusion.1, f32[64,16384]{1,0:T(8,128)S(1)} %copy-done), kind=kOutput, calls=%fused_computation.1 | convolution fusion | flops 807403520 | bytes 12599296 | tf_op jit(solution)/shard_map/dot_general | solution.py:33
  (98 shorter events, 16.4 us)
Async XLA Ops:
  15.0 27.5 %all-to-all-start = ((f32[32,1,4096]{2,1,0:T(1,128)}), f32[32,1,4096]{2,1,0:T(1,128)S(1)}, u32[]{:S(2)}, u32[]{:S(2)}) async-start(f32[32,1,4096]{2,1,0:T(1,128)} %reshape.21), calls=%async_computation | async-start | bytes 1048576 | tf_op jit(solution)/shard_map/all_to_all | solution.py:17
  26.3 193.6 %all-gather.5.cloned.1.call-start = ((), (), s32[]{:S(2)}) async-start(), calls=%async_computation.4 | async-start | bytes 20971520 | tf_op jit(solution)/shard_map/all_gather | solution.py:28
  67.0 190.8 %all-gather.7.cloned.1.call-start = ((), (), s32[]{:S(2)}) async-start(), calls=%async_computation.5 | async-start | bytes 12582912 | tf_op jit(solution)/shard_map/all_gather | solution.py:28
  264.2 18.3 %copy-start.1 = (s32[8]{0:T(128)S(1)}, s32[8]{0:T(128)}, u32[]{:S(2)}) copy-start(s32[8]{0:T(128)} %param.6) | copy-start | bytes 100
  272.7 26.2 %all-to-all-start.1 = ((f32[32,1,4096]{2,1,0:T(1,128)}), f32[32,1,4096]{2,1,0:T(1,128)S(1)}, u32[]{:S(2)}, u32[]{:S(2)}) async-start(f32[32,1,4096]{2,1,0:T(1,128)} %reshape.23), calls=%async_computation.1 | async-start | bytes 1048576 | tf_op jit(solution)/shard_map/all_to_all | solution.py:17
  282.3 123.6 %all-reduce.2.cloned.1.call-start = ((), (), s32[]{:S(2)}) async-start(), calls=%async_computation.3 | async-start | bytes 8388608 | tf_op jit(solution)/shard_map/psum | solution.py:65
  446.8 8.7 %copy-start = (f32[64,16384]{1,0:T(8,128)S(1)}, f32[64,16384]{1,0:T(8,128)}, u32[]{:S(2)}) copy-start(f32[64,16384]{1,0:T(8,128)} %all-reduce.2.cloned.1.call-done) | copy-start | bytes 12582916
Sparse Core Ops, SparseCore 0:
  67.1 152.7 all-gather.4
  229.3 28.3 all-gather.6
  331.3 74.6 all-reduce.1
